TPU v7x, 512 devices: a whole 4x8x8 slice. The times are simulated.
512 devices in a mesh: seq: 64 (over z_lo, y, x), res: 8 (over z_hi, core).
Axes of the slice: x: 4, y: 8, z: 8 (z_hi: 4, z_lo: 2; z = z_hi * 2 + z_lo), core: 2. Of those that a mesh axis runs over, the one named last changes fastest.
Arguments:
- alignment_tensor: bfloat16 [256, 1024, 256], P('seq', 'res'), may hold values from -6 to 6
- scaling_entries: float32 [256], replicated, may hold values from 0.1 to 1.9
- probe_matrix: bfloat16 [256, 256], replicated, may hold values from -0.375 to 0.375
- lookup_matrix: bfloat16 [256, 256], replicated, may hold values from -0.75 to 0.75
- content_matrix: bfloat16 [256, 256], replicated, may hold values from -0.375 to 0.375
- gating_matrix: bfloat16 [256, 256], replicated, may hold values from -0.375 to 0.375
- final_projection_matrix: bfloat16 [256, 256], replicated, may hold values from -1.5 to 1.5
- residue_offset_logits: bfloat16 [8, 1024, 1024], P(None, 'res', 'seq'), may hold values from -10 to 250
Outputs:
- update: bfloat16 [256, 1024, 256], P('seq', 'res')
All inputs are finite; a program needn't handle non-finite values.
Results may differ from a plain program's by a relative error of at most 0.012.
Values may be sent and summed in bfloat16 or wider, within the bound.
A program may use at most 64 MiB of HBM per device.

v0:
```python
import jax
import jax.numpy as jnp
from jax import lax
from jax.sharding import PartitionSpec as P


def standardize_features(alignment_tensor, scaling_entries):
    content_entries = alignment_tensor.astype(jnp.float32)
    center = jnp.mean(content_entries, axis=-1, keepdims=True)
    variance = jnp.mean((content_entries - center) ** 2, axis=-1, keepdims=True)
    return ((content_entries - center) * lax.rsqrt(variance + 1e-05) * scaling_entries).astype(
        jnp.bfloat16
    )


def on_device(
    alignment_tensor,
    scaling_entries,
    probe_matrix,
    lookup_matrix,
    content_matrix,
    gating_matrix,
    final_projection_matrix,
    residue_offset_logits,
):
    shard_homologs, shard_alignment, feature_depth = alignment_tensor.shape
    head_count = residue_offset_logits.shape[0]
    head_size = feature_depth // head_count
    standardized_alignment = standardize_features(alignment_tensor, scaling_entries)
    flat_rows = standardized_alignment.reshape(-1, feature_depth)
    queries = (
        jnp.dot(flat_rows, probe_matrix, preferred_element_type=jnp.float32) * head_size ** (-0.5)
    ).astype(jnp.bfloat16)
    queries = queries.reshape(shard_homologs, shard_alignment, feature_depth)
    sigmoid_factors = jax.nn.sigmoid(
        jnp.dot(flat_rows, gating_matrix, preferred_element_type=jnp.float32)
    )
    piece_rows = standardized_alignment.reshape(-1, feature_depth)
    key_part = jnp.dot(piece_rows, lookup_matrix, preferred_element_type=jnp.float32).astype(
        jnp.bfloat16
    )
    value_part = jnp.dot(piece_rows, content_matrix, preferred_element_type=jnp.float32).astype(
        jnp.bfloat16
    )
    key_values = lax.all_gather(
        jnp.stack(
            [
                key_part.reshape(standardized_alignment.shape),
                value_part.reshape(standardized_alignment.shape),
            ]
        ),
        "res",
        axis=2,
        tiled=True,
    )
    total_keys = key_values.shape[2]
    block_width = min(512, total_keys)
    block_count = total_keys // block_width

    def attend_head(head_number):
        low = head_number * head_size
        query_head = queries[:, :, low : low + head_size]
        key_head = key_values[0][:, :, low : low + head_size]
        value_head = key_values[1][:, :, low : low + head_size]
        bias_head = lax.all_gather(residue_offset_logits[head_number], "seq", axis=1, tiled=True)

        def step(carry, block_number):
            running_max, denominator, weighted = carry
            first_col = block_number * block_width
            key_block = lax.dynamic_slice_in_dim(key_head, first_col, block_width, 1)
            value_block = lax.dynamic_slice_in_dim(value_head, first_col, block_width, 1)
            bias_block = lax.dynamic_slice_in_dim(bias_head, first_col, block_width, 1)
            scores = jnp.einsum(
                "sid,sjd->sij", query_head, key_block, preferred_element_type=jnp.float32
            )
            scores = scores + bias_block.astype(jnp.float32)[None]
            new_max = jnp.maximum(running_max, jnp.max(scores, axis=-1))
            rescale = jnp.exp(running_max - new_max)
            expo = jnp.exp(scores - new_max[..., None])
            denominator = denominator * rescale + jnp.sum(expo, axis=-1)
            contrib = jnp.einsum(
                "sij,sjd->sid",
                expo.astype(jnp.bfloat16),
                value_block,
                preferred_element_type=jnp.float32,
            )
            weighted = weighted * rescale[..., None] + contrib
            return ((new_max, denominator, weighted), None)

        start_state = (
            jnp.full((shard_homologs, shard_alignment), -1e30, jnp.float32),
            jnp.zeros((shard_homologs, shard_alignment), jnp.float32),
            jnp.zeros((shard_homologs, shard_alignment, head_size), jnp.float32),
        )
        final_state, unused = lax.scan(step, start_state, jnp.arange(block_count))
        return final_state[2] / final_state[1][..., None]

    head_results = [attend_head(head_number) for head_number in range(head_count)]
    attention_mixture = jnp.concatenate(head_results, axis=2).reshape(-1, feature_depth)
    modulated_mixture = (attention_mixture * sigmoid_factors).astype(jnp.bfloat16)
    update = jnp.dot(
        modulated_mixture, final_projection_matrix, preferred_element_type=jnp.float32
    ).astype(jnp.bfloat16)
    return update.reshape(shard_homologs, shard_alignment, feature_depth)


def solution(mesh):
    return jax.shard_map(
        on_device,
        mesh=mesh,
        in_specs=(P("seq", "res", None), P(), P(), P(), P(), P(), P(), P(None, "res", "seq")),
        out_specs=P("seq", "res", None),
        check_vma=False,
    )
```

profile of v0, /device:TPU:130, one launch (start us, length us, event | category | flops | bytes accessed | tf_op | source)
XLA Modules:
  0.0 1436.9 jit_solution(11572056241382402710)
XLA Ops:
  18.1 163.9 %all-gather.7 = bf16[1,128,1024]{1,2,0:T(8,128)(2,1)} all-gather(bf16[1,128,16]{1,2,0:T(8,128)(2,1)S(1)} %get-tuple-element.847), channel_id=9, replica_groups=mesh['seq'=64,'res'=8] {'seq'}, dimensions={2}, use_global_device_ids=true | all-gather | bytes 266240 | tf_op jit(solution)/shard_map/all_gather | solution.py:65
  182.0 166.8 %all-gather.6 = bf16[1,128,1024]{1,2,0:T(8,128)(2,1)} all-gather(bf16[1,128,16]{1,2,0:T(8,128)(2,1)S(1)} %get-tuple-element.854), channel_id=8, replica_groups=mesh['seq'=64,'res'=8] {'seq'}, dimensions={2}, use_global_device_ids=true | all-gather | bytes 266240 | tf_op jit(solution)/shard_map/all_gather | solution.py:65
  348.8 161.1 %all-gather.5 = bf16[1,128,1024]{1,2,0:T(8,128)(2,1)} all-gather(bf16[1,128,16]{1,2,0:T(8,128)(2,1)S(1)} %get-tuple-element.848), channel_id=7, replica_groups=mesh['seq'=64,'res'=8] {'seq'}, dimensions={2}, use_global_device_ids=true | all-gather | bytes 266240 | tf_op jit(solution)/shard_map/all_gather | solution.py:65
  509.9 163.1 %all-gather.4 = bf16[1,128,1024]{1,2,0:T(8,128)(2,1)} all-gather(bf16[1,128,16]{1,2,0:T(8,128)(2,1)S(1)} %get-tuple-element.849), channel_id=6, replica_groups=mesh['seq'=64,'res'=8] {'seq'}, dimensions={2}, use_global_device_ids=true | all-gather | bytes 266240 | tf_op jit(solution)/shard_map/all_gather | solution.py:65
  673.0 161.1 %all-gather.3 = bf16[1,128,1024]{1,2,0:T(8,128)(2,1)} all-gather(bf16[1,128,16]{1,2,0:T(8,128)(2,1)S(1)} %get-tuple-element.850), channel_id=5, replica_groups=mesh['seq'=64,'res'=8] {'seq'}, dimensions={2}, use_global_device_ids=true | all-gather | bytes 266240 | tf_op jit(solution)/shard_map/all_gather | solution.py:65
  834.1 163.1 %all-gather.2 = bf16[1,128,1024]{1,2,0:T(8,128)(2,1)} all-gather(bf16[1,128,16]{1,2,0:T(8,128)(2,1)S(1)} %get-tuple-element.851), channel_id=4, replica_groups=mesh['seq'=64,'res'=8] {'seq'}, dimensions={2}, use_global_device_ids=true | all-gather | bytes 266240 | tf_op jit(solution)/shard_map/all_gather | solution.py:65
  997.2 161.1 %all-gather.1 = bf16[1,128,1024]{1,2,0:T(8,128)(2,1)} all-gather(bf16[1,128,16]{1,2,0:T(8,128)(2,1)S(1)} %get-tuple-element.852), channel_id=3, replica_groups=mesh['seq'=64,'res'=8] {'seq'}, dimensions={2}, use_global_device_ids=true | all-gather | bytes 266240 | tf_op jit(solution)/shard_map/all_gather | solution.py:65
  1158.3 163.3 %all-gather = bf16[1,128,1024]{1,2,0:T(8,128)(2,1)} all-gather(bf16[1,128,16]{1,2,0:T(8,128)(2,1)S(1)} %get-tuple-element.853), channel_id=2, replica_groups=mesh['seq'=64,'res'=8] {'seq'}, dimensions={2}, use_global_device_ids=true | all-gather | bytes 266240 | tf_op jit(solution)/shard_map/all_gather | solution.py:65
  1321.5 2.7 slice_bitcast_fusion
  1326.3 14.9 %while.127 = (s32[]{:T(128)}, f32[4,128]{1,0:T(4,128)}, f32[4,128]{1,0:T(4,128)}, f32[4,128,32]{1,2,0:T(8,128)}, s32[2]{0:T(128)}, /*index=5*/bf16[4,1024,32]{1,...) while((s32[]{:T(128)}, f32[4,128]{1,0:T(4,128)}, ...), condition=%wide.region_33.34_spmd.clone, body=%wide.region_30.33_spmd.clone.sunk | while | flops 35244548 | bytes 4260047 | solution.py:95
  1338.8 1.7 convolution_add_fusion.23
  1343.4 15.0 %while.126 = (s32[]{:T(128)}, f32[4,128]{1,0:T(4,128)}, f32[4,128]{1,0:T(4,128)}, f32[4,128,32]{1,2,0:T(8,128)}, s32[2]{0:T(128)}, /*index=5*/bf16[4,1024,32]{1,...) while((s32[]{:T(128)}, f32[4,128]{1,0:T(4,128)}, ...), condition=%wide.region_29.30_spmd.clone, body=%wide.region_26.29_spmd.clone.sunk | while | flops 35244548 | bytes 4260047 | solution.py:95
  1356.1 1.7 convolution_add_fusion.22
  1358.4 1.7 copy.50
  1360.7 13.4 while.125
  1371.7 1.8 convolution_add_fusion.21
  1376.4 13.5 while.124
  1387.5 1.8 convolution_add_fusion.20
  1392.1 13.0 while.123
  1402.7 1.8 convolution_add_fusion.19
  1405.0 1.7 copy.44
  1406.8 7.4 while.122
  1415.9 4.4 while.121
  1421.3 4.4 while.120
  (280 shorter events, 93.5 us)
Async XLA Ops:
  6.5 1315.0 %all-gather.10.cloned.1.call-start = ((), (), s32[]{:S(2)}) async-start(), calls=%async_computation | async-start | bytes 4718592 | tf_op jit(solution)/shard_map/all_gather | solution.py:45
  11.8 6.3 copy-start.35
  1343.4 17.3 %copy-start.6 = (bf16[1,128,1024]{1,2,0:T(8,128)(2,1)S(1)}, bf16[1,128,1024]{1,2,0:T(8,128)(2,1)}, u32[]{:S(2)}) copy-start(bf16[1,128,1024]{1,2,0:T(8,128)(2,1)} %all-gather.5) | copy-start | bytes 786436
  1360.7 15.6 %copy-start.5 = (bf16[1,128,1024]{1,2,0:T(8,128)(2,1)S(1)}, bf16[1,128,1024]{1,2,0:T(8,128)(2,1)}, u32[]{:S(2)}) copy-start(bf16[1,128,1024]{1,2,0:T(8,128)(2,1)} %all-gather.4) | copy-start | bytes 786436
  1376.4 15.7 %copy-start.4 = (bf16[1,128,1024]{1,2,0:T(8,128)(2,1)S(1)}, bf16[1,128,1024]{1,2,0:T(8,128)(2,1)}, u32[]{:S(2)}) copy-start(bf16[1,128,1024]{1,2,0:T(8,128)(2,1)} %all-gather.3) | copy-start | bytes 786436
  1376.4 15.7 %copy-start.10 = (bf16[4,1024,32]{1,2,0:T(8,128)(2,1)S(1)}, bf16[4,1024,32]{1,2,0:T(8,128)(2,1)}, u32[]{:S(2)}) copy-start(bf16[4,1024,32]{1,2,0:T(8,128)(2,1)} %get-tuple-element.1489) | copy-start | bytes 786436
  1392.1 14.7 %copy-start.3 = (bf16[1,128,1024]{1,2,0:T(8,128)(2,1)S(1)}, bf16[1,128,1024]{1,2,0:T(8,128)(2,1)}, u32[]{:S(2)}) copy-start(bf16[1,128,1024]{1,2,0:T(8,128)(2,1)} %all-gather.2) | copy-start | bytes 786436
  1392.1 14.7 %copy-start.9 = (bf16[4,1024,32]{1,2,0:T(8,128)(2,1)S(1)}, bf16[4,1024,32]{1,2,0:T(8,128)(2,1)}, u32[]{:S(2)}) copy-start(bf16[4,1024,32]{1,2,0:T(8,128)(2,1)} %get-tuple-element.1450) | copy-start | bytes 786436
  1406.7 9.1 copy-start.2
  1406.7 9.1 copy-start.8
  1406.7 9.1 copy-start.12
  1406.8 9.1 copy-start.16
  1406.8 9.1 copy-start.26
  1415.9 5.3 copy-start.1
  1415.9 5.3 copy-start.7
  1415.9 5.3 copy-start.11
  1415.9 5.3 copy-start.15
  1415.9 5.3 copy-start.25
  1421.2 4.6 copy-start.17
  1421.2 4.8 copy-start.18
  1421.2 4.8 copy-start.33
  1421.2 4.9 copy-start.19
  1421.2 4.9 copy-start.32
  1421.2 5.1 copy-start.31
  (19 other events, 39.6 us)
Sparse Core Ops, SparseCore 0:
  11.9 63.2 all-gather.9
where the time goes:
time: 1440 us
  blocking collectives  1300 us (90%)
  local copies, waits for them, and re-layouts  49 us (3%)
  matrix products  33.1 us (2%)
  other arithmetic  26.2 us (2%)
    all_gather x8, blocking collectives, attend_head(): lax.all_gather(residue_offset_logits[head_number], 'seq', axis=1, tiled=T...  1300 us
  transfers between devices with their start and end apart: 1, of which 0 were waited for; matrix products, arithmetic and copies ran while one was open for 0% of the time, Pallas kernels for 0%

commit v1 on v0

v1 whole, which is shorter than its diff:
```python
import functools

import jax
import jax.numpy as jnp
from jax import lax
from jax.experimental import pallas as pl
from jax.experimental.pallas import tpu as pltpu
from jax.sharding import PartitionSpec as P

MESH = pl.DeviceIdType.MESH
BF16, F32 = jnp.bfloat16, jnp.float32
SEQS, ROWS, WIDTH, HEADS, HEAD = 4, 128, 256, 8, 32
PAIRS, BLOCK = HEADS // 2, 2 * ROWS
NX, NY, NZL, NZH = 4, 8, 2, 4
AUG = 80
NEG = -1e30


def dot(a, b):
    return jnp.dot(a, b, preferred_element_type=F32)


def dot_nt(a, b):
    return lax.dot_general(a, b, (((1,), (1,)), ((), ())), preferred_element_type=F32)


def normalise(rows, gain):
    wide = rows.astype(F32)
    center = jnp.mean(wide, axis=-1, keepdims=True)
    moved = wide - center
    variance = jnp.mean(moved * moved, axis=-1, keepdims=True)
    return (moved * lax.rsqrt(variance + 1e-05) * gain).astype(BF16)


def query_side(xn, wq, wg, qz, gt):
    wqt, wgt = wq[...].T, wg[...].T
    qz[...] = jnp.zeros_like(qz)
    for s in range(SEQS):
        rows = xn(s)
        qt = (dot_nt(wqt, rows) * HEAD**-0.5).astype(BF16)
        for h in range(HEADS):
            p, half = h // 2, h % 2
            qz[s, p, h * HEAD : (h + 1) * HEAD, half * ROWS : (half + 1) * ROWS] = qt[
                h * HEAD : (h + 1) * HEAD
            ]
        gt[s] = jax.nn.sigmoid(dot_nt(wgt, rows))


def key_side(xg, zh, core, c, slot, wk, wvt, kbuf, vt):
    wvt_all = wvt[...]
    for s in range(SEQS):
        rows = xg[zh, core, s]
        kbuf[slot, s, c * ROWS : (c + 1) * ROWS, :] = dot(rows, wk[...]).astype(BF16)
        values = dot_nt(wvt_all, rows).astype(BF16)
        for p in range(PAIRS):
            vt[slot, s, p, : 2 * HEAD, c * ROWS : (c + 1) * ROWS] = values[
                2 * HEAD * p : 2 * HEAD * (p + 1)
            ]


def bias_block(bta, btb, h, zl, ys):
    pieces = []
    for y in ys:
        for x in range(NX):
            if h < HEADS // 2:
                pieces.append(bta[y, zl, x, h])
            else:
                pieces.append(btb[x, zl, y, h - HEADS // 2])
    return jnp.concatenate(pieces, axis=0).astype(F32)


def attend(slot, zh, core, first, pairs, kbuf, vt, qz, bta, btb, m_ref, l_ref, acc):
    zl = zh // (NZH // NZL)
    y0 = lax.rem(zh, NZH // NZL) * (NY // 2)
    ys = [y0 + 2 * core, y0 + 2 * core + 1, y0 + 2 * (1 - core), y0 + 2 * (1 - core) + 1]

    def body(s, carry):
        keys = kbuf[slot, s]
        for p in pairs:
            scores = dot(keys, qz[s, p])
            scores = scores + jnp.concatenate(
                [bias_block(bta, btb, 2 * p + i, zl, ys) for i in range(2)], axis=1
            )
            top = jnp.max(scores, axis=0, keepdims=True)
            if not first:
                old = m_ref[s, p]
                top = jnp.maximum(old, top)
            weights = jnp.exp(scores - top).astype(BF16)
            mixed = dot(vt[slot, s, p], weights)
            total = mixed[2 * HEAD : 2 * HEAD + 1]
            left, right = mixed[:HEAD, :ROWS], mixed[HEAD : 2 * HEAD, ROWS:]
            if not first:
                scale = jnp.exp(old - top)
                total = l_ref[s, p] * scale + total
                left = acc[s, p, 0] * scale[:, :ROWS] + left
                right = acc[s, p, 1] * scale[:, ROWS:] + right
            m_ref[s, p] = top
            l_ref[s, p] = total
            acc[s, p, 0] = left
            acc[s, p, 1] = right
        return carry

    lax.fori_loop(0, SEQS, body, 0)


def finish(wo, gt, l_ref, acc, out):
    for s in range(SEQS):
        parts = []
        for p in range(PAIRS):
            for half in range(2):
                h = 2 * p + half
                total = l_ref[s, p, :, half * ROWS : (half + 1) * ROWS]
                parts.append(acc[s, p, half] / total * gt[s, h * HEAD : (h + 1) * HEAD])
        gated = jnp.concatenate(parts, axis=0).astype(BF16)
        out[s] = dot(gated.T, wo[...]).astype(BF16)


def kernel(
    x_hbm, gain_hbm, wq_hbm, wk_hbm, wv_hbm, wg_hbm, wo_hbm, b_hbm, out,
    x, gain, wq, wk, wv, wg, wo, b,
    xg, bta, btb, wvt, kbuf, vt, qz, gt, m_ref, l_ref, acc,
    local, xs, xr, as_, ar, bs, br,
):
    seq, res = lax.axis_index("seq"), lax.axis_index("res")
    zl, y, xx = seq // (NY * NX), lax.rem(seq // NX, NY), lax.rem(seq, NX)
    zh, core = res // 2, lax.rem(res, 2)

    def at_seq(zl_, y_, x_):
        return (zl_ * (NY * NX) + y_ * NX + x_, res)

    def at_res(zh_, core_):
        return (seq, zh_ * 2 + core_)

    def mod(v, n):
        return lax.rem(v + n, n)

    z_next, z_prev = mod(zh + 1, NZH), mod(zh - 1, NZH)
    y_next, y_prev = mod(y + 1, NY), mod(y - 1, NY)
    x_next, x_prev = mod(xx + 1, NX), mod(xx - 1, NX)
    dev_zn, dev_zp, dev_sib = at_res(z_next, core), at_res(z_prev, core), at_res(zh, 1 - core)
    dev_yn, dev_yp = at_seq(zl, y_next, xx), at_seq(zl, y_prev, xx)
    dev_xn, dev_xp = at_seq(zl, y, x_next), at_seq(zl, y, x_prev)
    dev_zl = at_seq(1 - zl, y, xx)

    barrier = pltpu.get_barrier_semaphore()
    peers = (dev_zn, dev_zp, dev_sib, dev_yn, dev_yp, dev_xn, dev_xp, dev_zl)
    for peer in peers:
        pl.semaphore_signal(barrier, inc=1, device_id=peer, device_id_type=MESH)

    loads = [
        pltpu.make_async_copy(src, dst, local.at[i])
        for i, (src, dst) in enumerate(
            [(x_hbm, x), (gain_hbm, gain), (b_hbm, b), (wk_hbm, wk), (wv_hbm, wv), (wq_hbm, wq), (wg_hbm, wg), (wo_hbm, wo)]
        )
    ]
    for load in loads:
        load.start()
    loads[0].wait()
    loads[1].wait()
    for s in range(SEQS):
        xg[zh, core, s] = normalise(x[s], gain[...])
    loads[2].wait()
    half_heads = HEADS // 2
    bta[y, zl, xx] = b[:half_heads]
    btb[xx, zl, y] = b[half_heads:]

    started = []

    def send(ref, dev, sems, i):
        copy = pltpu.make_async_remote_copy(
            src_ref=ref, dst_ref=ref, send_sem=sems[0].at[i], recv_sem=sems[1].at[i],
            device_id=dev, device_id_type=MESH,
        )
        copy.start()
        started.append(copy)

    def arrive(ref, sems, i):
        pltpu.make_async_remote_copy(
            src_ref=ref, dst_ref=ref, send_sem=sems[0].at[i], recv_sem=sems[1].at[i],
            device_id=dev_sib, device_id_type=MESH,
        ).wait_recv()

    sx, sa, sb = (xs, xr), (as_, ar), (bs, br)
    lo, hi = pl.ds(0, 2), pl.ds(2, 2)

    pl.semaphore_wait(barrier, len(peers))

    send(bta.at[y, zl, xx], dev_zl, sa, 0)
    send(btb.at[xx, zl, y], dev_zl, sb, 0)
    send(xg.at[zh, core, lo], dev_zn, sx, 0)
    send(xg.at[zh, core, hi], dev_zp, sx, 1)
    send(xg.at[zh, core, hi], dev_zn, sx, 2)
    send(xg.at[zh, core, lo], dev_zp, sx, 3)
    send(xg.at[zh, core], dev_sib, sx, 4)

    arrive(bta.at[y, 1 - zl, xx], sa, 0)
    send(bta.at[y, :, xx], dev_xn, sa, 1)
    send(bta.at[y, :, xx], dev_xp, sa, 2)
    arrive(btb.at[xx, 1 - zl, y], sb, 0)
    send(btb.at[xx, :, y], dev_yn, sb, 1)
    send(btb.at[xx, :, y], dev_yp, sb, 2)

    loads[3].wait()
    loads[4].wait()
    wvt[...] = wv[...].T
    ones = jnp.ones((AUG - 2 * HEAD, BLOCK), BF16)
    for slot in range(NZH):
        for s in range(SEQS):
            for p in range(PAIRS):
                vt[slot, s, p, 2 * HEAD :] = ones

    arrive(bta.at[y, :, x_prev], sa, 1)
    send(bta.at[y, 0, x_prev], dev_xn, sa, 3)
    arrive(bta.at[y, :, x_next], sa, 2)
    send(bta.at[y, 1, x_next], dev_xp, sa, 4)
    arrive(btb.at[xx, :, y_prev], sb, 1)
    send(btb.at[xx, :, y_prev], dev_yn, sb, 3)
    arrive(btb.at[xx, :, y_next], sb, 2)
    send(btb.at[xx, :, y_next], dev_yp, sb, 4)

    loads[5].wait()
    loads[6].wait()

    x_opp = mod(xx + 2, NX)
    arrive(bta.at[y, 0, x_opp], sa, 3)
    arrive(bta.at[y, 1, x_opp], sa, 4)
    send(bta.at[y], dev_yn, sa, 5)
    send(bta.at[y], dev_yp, sa, 6)
    query_side(lambda s: xg[zh, core, s], wq, wg, qz, gt)

    y_prev2, y_next2 = mod(y - 2, NY), mod(y + 2, NY)
    y_prev3, y_next3 = mod(y - 3, NY), mod(y + 3, NY)
    y_opp = mod(y + 4, NY)
    arrive(btb.at[xx, :, y_prev2], sb, 3)
    send(btb.at[xx, :, y_prev2], dev_yn, sb, 5)
    arrive(btb.at[xx, :, y_next2], sb, 4)
    send(btb.at[xx, :, y_next2], dev_yp, sb, 6)
    key_side(xg, zh, core, 0, 0, wk, wvt, kbuf, vt)
    arrive(btb.at[xx, :, y_prev3], sb, 5)
    send(btb.at[xx, 0, y_prev3], dev_yn, sb, 7)
    arrive(btb.at[xx, :, y_next3], sb, 6)
    send(btb.at[xx, 1, y_next3], dev_yp, sb, 8)
    arrive(bta.at[y_prev], sa, 5)
    send(bta.at[y_prev], dev_yn, sa, 7)
    arrive(bta.at[y_next], sa, 6)
    send(bta.at[y_next], dev_yp, sa, 8)
    arrive(btb.at[xx, 0, y_opp], sb, 7)
    arrive(btb.at[xx, 1, y_opp], sb, 8)
    send(btb.at[xx], dev_xn, sb, 9)
    send(btb.at[xx], dev_xp, sb, 10)

    arrive(xg.at[z_prev, core, lo], sx, 0)
    send(xg.at[z_prev, core, lo], dev_zn, sx, 5)
    send(xg.at[z_prev, core, lo], dev_sib, sx, 7)
    arrive(xg.at[z_next, core, hi], sx, 1)
    send(xg.at[z_next, core, hi], dev_zp, sx, 6)
    send(xg.at[z_next, core, hi], dev_sib, sx, 8)
    arrive(bta.at[y_prev2], sa, 7)
    send(bta.at[y_prev2], dev_yn, sa, 9)
    arrive(bta.at[y_next2], sa, 8)
    send(bta.at[y_next2], dev_yp, sa, 10)
    arrive(xg.at[zh, 1 - core], sx, 4)
    key_side(xg, zh, 1 - core, 1, 0, wk, wvt, kbuf, vt)
    arrive(bta.at[y_prev3], sa, 9)
    send(bta.at[y_prev3, 0], dev_yn, sa, 11)
    arrive(bta.at[y_next3], sa, 10)
    send(bta.at[y_next3, 1], dev_yp, sa, 12)
    arrive(btb.at[x_prev], sb, 9)
    send(btb.at[x_prev, 0], dev_xn, sb, 11)
    arrive(btb.at[x_next], sb, 10)
    send(btb.at[x_next, 1], dev_xp, sb, 12)

    arrive(xg.at[z_prev, core, hi], sx, 2)
    send(xg.at[z_prev, core, hi], dev_sib, sx, 9)
    arrive(xg.at[z_next, core, lo], sx, 3)
    send(xg.at[z_next, core, lo], dev_sib, sx, 10)
    key_side(xg, z_prev, core, 0, 1, wk, wvt, kbuf, vt)
    key_side(xg, z_next, core, 0, 2, wk, wvt, kbuf, vt)
    arrive(xg.at[z_prev, 1 - core, lo], sx, 7)
    arrive(xg.at[z_prev, 1 - core, hi], sx, 9)
    key_side(xg, z_prev, 1 - core, 1, 1, wk, wvt, kbuf, vt)
    arrive(xg.at[z_next, 1 - core, hi], sx, 8)
    arrive(xg.at[z_next, 1 - core, lo], sx, 10)
    key_side(xg, z_next, 1 - core, 1, 2, wk, wvt, kbuf, vt)

    arrive(bta.at[y_opp, 0], sa, 11)
    arrive(bta.at[y_opp, 1], sa, 12)
    arrive(btb.at[x_opp, 0], sb, 11)
    arrive(btb.at[x_opp, 1], sb, 12)
    state = (kbuf, vt, qz, bta, btb, m_ref, l_ref, acc)
    pairs = range(PAIRS)
    attend(0, zh, core, True, pairs, *state)
    z_opp = mod(zh + 2, NZH)
    arrive(xg.at[z_opp, core, lo], sx, 5)
    send(xg.at[z_opp, core, lo], dev_sib, sx, 11)
    arrive(xg.at[z_opp, core, hi], sx, 6)
    send(xg.at[z_opp, core, hi], dev_sib, sx, 12)
    attend(1, z_prev, core, False, pairs, *state)
    attend(2, z_next, core, False, pairs, *state)
    key_side(xg, z_opp, core, 0, 3, wk, wvt, kbuf, vt)
    arrive(xg.at[z_opp, 1 - core, lo], sx, 11)
    arrive(xg.at[z_opp, 1 - core, hi], sx, 12)
    key_side(xg, z_opp, 1 - core, 1, 3, wk, wvt, kbuf, vt)
    attend(3, z_opp, core, False, pairs, *state)
    loads[7].wait()
    finish(wo, gt, l_ref, acc, out)
    for copy in started:
        copy.wait_send()


def scratch():
    sem = pltpu.SemaphoreType.DMA
    mat = pltpu.VMEM((WIDTH, WIDTH), BF16)
    half = HEADS // 2
    return [
        pltpu.VMEM((SEQS, ROWS, WIDTH), BF16),
        pltpu.VMEM((1, WIDTH), F32),
        mat, mat, mat, mat, mat,
        pltpu.VMEM((HEADS, 16, ROWS), BF16),
        pltpu.VMEM((NZH, 2, SEQS, ROWS, WIDTH), BF16),
        pltpu.VMEM((NY, NZL, NX, half, 16, ROWS), BF16),
        pltpu.VMEM((NX, NZL, NY, half, 16, ROWS), BF16),
        mat,
        pltpu.VMEM((NZH, SEQS, BLOCK, WIDTH), BF16),
        pltpu.VMEM((NZH, SEQS, PAIRS, AUG, BLOCK), BF16),
        pltpu.VMEM((SEQS, PAIRS, WIDTH, BLOCK), BF16),
        pltpu.VMEM((SEQS, WIDTH, ROWS), F32),
        pltpu.VMEM((SEQS, PAIRS, 1, BLOCK), F32),
        pltpu.VMEM((SEQS, PAIRS, 1, BLOCK), F32),
        pltpu.VMEM((SEQS, PAIRS, 2, HEAD, ROWS), F32),
        sem((8,)),
        sem((13,)), sem((13,)), sem((13,)), sem((13,)), sem((13,)), sem((13,)),
    ]


def on_device(x, gain, wq, wk, wv, wg, wo, b):
    any_space = pl.BlockSpec(memory_space=pltpu.HBM)
    return pl.pallas_call(
        kernel,
        out_shape=jax.ShapeDtypeStruct(x.shape, x.dtype),
        in_specs=[any_space] * 8,
        out_specs=pl.BlockSpec(memory_space=pltpu.VMEM),
        scratch_shapes=scratch(),
        compiler_params=pltpu.CompilerParams(
            collective_id=0, has_side_effects=True, vmem_limit_bytes=48 * 1024 * 1024
        ),
        cost_estimate=pl.CostEstimate(flops=6 * 10**9, bytes_accessed=2 * 10**6, transcendentals=5 * 10**6),
    )(x, gain.reshape(1, -1), wq, wk, wv, wg, wo, jnp.swapaxes(b, 1, 2))


def solution(mesh):
    return jax.shard_map(
        on_device,
        mesh=mesh,
        in_specs=(P("seq", "res", None), P(), P(), P(), P(), P(), P(), P(None, "res", "seq")),
        out_specs=P("seq", "res", None),
        check_vma=False,
    )
```

time: 1440 us -> 75.6 us (0.05)
  the two profiles are of different devices: /device:TPU:130 before, /device:TPU:16 now
where the time goes in v1:
time: 75.6 us; the launch traced here: 75.2 us
  Pallas kernels  67.6 us (89%)
  local copies, waits for them, and re-layouts  7.61 us (10%)
    pallas_call x1, Pallas kernels, on_device(): pl.pallas_call(kernel, out_shape=jax.ShapeDtypeStruct(x.shape, x.dtype),...  67.6 us
    unnamed x17, local copies, waits for them, and re-layouts  7.61 us

profile of v1, /device:TPU:16, one launch (start us, length us, event | category | flops | bytes accessed | tf_op | source)
XLA Modules:
  0.0 75.2 jit_solution(8745458919511221757)
XLA Ops:
  0.0 0.0 copy-start.7
  0.0 0.7 copy-done.7
  0.7 0.0 copy-start
  0.7 0.9 %copy-done = bf16[4,128,256]{2,1,0:T(8,128)(2,1)S(1)} copy-done((bf16[4,128,256]{2,1,0:T(8,128)(2,1)S(1)}, bf16[4,128,256]{2,1,0:T(8,128)(2,1)}, u32[]{:S(2)}) %copy-start) | copy-done | bytes 262168
  1.6 0.0 copy-start.1
  1.6 0.9 %copy-done.1 = bf16[256,256]{1,0:T(8,128)(2,1)S(1)} copy-done((bf16[256,256]{1,0:T(8,128)(2,1)S(1)}, bf16[256,256]{1,0:T(8,128)(2,1)}, u32[]{:S(2)}) %copy-start.1) | copy-done | bytes 131096
  2.5 0.0 copy-start.2
  2.5 0.9 %copy-done.2 = bf16[256,256]{1,0:T(8,128)(2,1)S(1)} copy-done((bf16[256,256]{1,0:T(8,128)(2,1)S(1)}, bf16[256,256]{1,0:T(8,128)(2,1)}, u32[]{:S(2)}) %copy-start.2) | copy-done | bytes 131096
  3.4 0.0 copy-start.3
  3.4 0.9 %copy-done.3 = bf16[256,256]{1,0:T(8,128)(2,1)S(1)} copy-done((bf16[256,256]{1,0:T(8,128)(2,1)S(1)}, bf16[256,256]{1,0:T(8,128)(2,1)}, u32[]{:S(2)}) %copy-start.3) | copy-done | bytes 131096
  4.3 0.0 copy-start.4
  4.3 0.9 %copy-done.4 = bf16[256,256]{1,0:T(8,128)(2,1)S(1)} copy-done((bf16[256,256]{1,0:T(8,128)(2,1)S(1)}, bf16[256,256]{1,0:T(8,128)(2,1)}, u32[]{:S(2)}) %copy-start.4) | copy-done | bytes 131096
  5.2 0.0 copy-start.5
  5.3 0.9 %copy-done.5 = bf16[256,256]{1,0:T(8,128)(2,1)S(1)} copy-done((bf16[256,256]{1,0:T(8,128)(2,1)S(1)}, bf16[256,256]{1,0:T(8,128)(2,1)}, u32[]{:S(2)}) %copy-start.5) | copy-done | bytes 131096
  6.2 0.0 copy-start.6
  6.2 0.8 %copy-done.6 = bf16[8,128,16]{1,2,0:T(8,128)(2,1)S(1)} copy-done((bf16[8,128,16]{1,2,0:T(8,128)(2,1)S(1)}, bf16[8,128,16]{1,2,0:T(8,128)(2,1)}, u32[]{:S(2)}) %copy-start.6) | copy-done | bytes 32792
  6.9 67.6 %shard_map.82 = bf16[4,128,256]{2,1,0:T(8,128)(2,1)S(1)} custom-call(bf16[4,128,256]{2,1,0:T(8,128)(2,1)S(1)} %copy-done, f32[1,256]{1,0:T(1,128)S(1)} %bitcast.3, bf16[256,256]{1,0:T(8,128)(2,1)S(1)} %copy-done.1, bf16[256,256]{1,0:T(8,128)(2,1)S(1)} %copy-done.2, bf16[256,256]{1,0:T(8,128)(2,1)S(1)} %copy-done.3, bf16[256,256]{1,0:T(8,128)(2,1)S(1)} %copy-done.4, ...), custom_call_target="tpu_custom_call" | custom-call | flops 6000000000 | bytes 2000000 | tf_op jit(solution)/shard_map/pallas_call | solution.py:338
  74.5 0.7 copy.10
Async XLA Ops:
  0.0 0.7 copy-start.7
  0.7 0.9 %copy-start = (bf16[4,128,256]{2,1,0:T(8,128)(2,1)S(1)}, bf16[4,128,256]{2,1,0:T(8,128)(2,1)}, u32[]{:S(2)}) copy-start(bf16[4,128,256]{2,1,0:T(8,128)(2,1)} %x_hbm.1) | copy-start | bytes 786436
  1.6 0.9 %copy-start.1 = (bf16[256,256]{1,0:T(8,128)(2,1)S(1)}, bf16[256,256]{1,0:T(8,128)(2,1)}, u32[]{:S(2)}) copy-start(bf16[256,256]{1,0:T(8,128)(2,1)} %wq_hbm.1) | copy-start | bytes 393220
  2.5 0.9 %copy-start.2 = (bf16[256,256]{1,0:T(8,128)(2,1)S(1)}, bf16[256,256]{1,0:T(8,128)(2,1)}, u32[]{:S(2)}) copy-start(bf16[256,256]{1,0:T(8,128)(2,1)} %wk_hbm.1) | copy-start | bytes 393220
  3.4 0.9 %copy-start.3 = (bf16[256,256]{1,0:T(8,128)(2,1)S(1)}, bf16[256,256]{1,0:T(8,128)(2,1)}, u32[]{:S(2)}) copy-start(bf16[256,256]{1,0:T(8,128)(2,1)} %wv_hbm.1) | copy-start | bytes 393220
  4.3 0.9 %copy-start.4 = (bf16[256,256]{1,0:T(8,128)(2,1)S(1)}, bf16[256,256]{1,0:T(8,128)(2,1)}, u32[]{:S(2)}) copy-start(bf16[256,256]{1,0:T(8,128)(2,1)} %wg_hbm.1) | copy-start | bytes 393220
  5.2 0.9 %copy-start.5 = (bf16[256,256]{1,0:T(8,128)(2,1)S(1)}, bf16[256,256]{1,0:T(8,128)(2,1)}, u32[]{:S(2)}) copy-start(bf16[256,256]{1,0:T(8,128)(2,1)} %wo_hbm.1) | copy-start | bytes 393220
  6.2 0.8 %copy-start.6 = (bf16[8,128,16]{1,2,0:T(8,128)(2,1)S(1)}, bf16[8,128,16]{1,2,0:T(8,128)(2,1)}, u32[]{:S(2)}) copy-start(bf16[8,128,16]{1,2,0:T(8,128)(2,1)} %param.15) | copy-start | bytes 98308

commit v2 on v1

--- a/solution.py
+++ b/solution.py
@@ -74,33 +74,48 @@
     y0 = lax.rem(zh, NZH // NZL) * (NY // 2)
     ys = [y0 + 2 * core, y0 + 2 * core + 1, y0 + 2 * (1 - core), y0 + 2 * (1 - core) + 1]
 
-    def body(s, carry):
-        keys = kbuf[slot, s]
-        for p in pairs:
-            scores = dot(keys, qz[s, p])
-            scores = scores + jnp.concatenate(
-                [bias_block(bta, btb, 2 * p + i, zl, ys) for i in range(2)], axis=1
-            )
+    def bias(p):
+        return jnp.concatenate([bias_block(bta, btb, 2 * p + i, zl, ys) for i in range(2)], axis=1)
+
+    def run(items):
+        n = len(items)
+        old, sc, w = [None] * n, [None] * n, [None] * n
+
+        def one(i):
+            s, p = items[i]
+            old[i] = None if first else (m_ref[s, p], l_ref[s, p], acc[s, p, 0], acc[s, p, 1])
+            sc[i] = dot(kbuf[slot, s], qz[s, p])
+
+        def two(i):
+            s, p = items[i]
+            scores = sc[i] + bias(p)
             top = jnp.max(scores, axis=0, keepdims=True)
             if not first:
-                old = m_ref[s, p]
-                top = jnp.maximum(old, top)
-            weights = jnp.exp(scores - top).astype(BF16)
+                top = jnp.maximum(old[i][0], top)
+            w[i] = (top, jnp.exp(scores - top).astype(BF16))
+
+        def three(i):
+            s, p = items[i]
+            top, weights = w[i]
             mixed = dot(vt[slot, s, p], weights)
             total = mixed[2 * HEAD : 2 * HEAD + 1]
             left, right = mixed[:HEAD, :ROWS], mixed[HEAD : 2 * HEAD, ROWS:]
             if not first:
-                scale = jnp.exp(old - top)
-                total = l_ref[s, p] * scale + total
-                left = acc[s, p, 0] * scale[:, :ROWS] + left
-                right = acc[s, p, 1] * scale[:, ROWS:] + right
-            m_ref[s, p] = top
-            l_ref[s, p] = total
-            acc[s, p, 0] = left
-            acc[s, p, 1] = right
-        return carry
-
-    lax.fori_loop(0, SEQS, body, 0)
+                scale = jnp.exp(old[i][0] - top)
+                total = old[i][1] * scale + total
+                left = old[i][2] * scale[:, :ROWS] + left
+                right = old[i][3] * scale[:, ROWS:] + right
+            m_ref[s, p], l_ref[s, p], acc[s, p, 0], acc[s, p, 1] = top, total, left, right
+
+        for t in range(n + 4):
+            if t < n:
+                one(t)
+            if 0 <= t - 2 < n:
+                two(t - 2)
+            if 0 <= t - 4 < n:
+                three(t - 4)
+
+    run([(s, p) for s in range(SEQS) for p in pairs])
 
 
 def finish(wo, gt, l_ref, acc, out):
@@ -119,7 +134,7 @@
     x_hbm, gain_hbm, wq_hbm, wk_hbm, wv_hbm, wg_hbm, wo_hbm, b_hbm, out,
     x, gain, wq, wk, wv, wg, wo, b,
     xg, bta, btb, wvt, kbuf, vt, qz, gt, m_ref, l_ref, acc,
-    local, xs, xr, as_, ar, bs, br,
+    local, ready, xs, xr, as_, ar, bs, br,
 ):
     seq, res = lax.axis_index("seq"), lax.axis_index("res")
     zl, y, xx = seq // (NY * NX), lax.rem(seq // NX, NY), lax.rem(seq, NX)
@@ -143,9 +158,19 @@
     dev_zl = at_seq(1 - zl, y, xx)
 
     barrier = pltpu.get_barrier_semaphore()
-    peers = (dev_zn, dev_zp, dev_sib, dev_yn, dev_yp, dev_xn, dev_xp, dev_zl)
-    for peer in peers:
-        pl.semaphore_signal(barrier, inc=1, device_id=peer, device_id_type=MESH)
+    partners = {
+        "zn": (dev_zn, zh < z_next, 1), "zp": (dev_zp, zh < z_prev, 0), "sib": (dev_sib, core < 1, 2),
+        "yn": (dev_yn, y < y_next, 4), "yp": (dev_yp, y < y_prev, 3), "xn": (dev_xn, xx < x_next, 6), "xp": (dev_xp, xx < x_prev, 5),
+        "zl": (dev_zl, zl < 1, 7),
+    }
+    slots = {name: i for i, name in enumerate(partners)}
+    late = 0
+    for dev, early, _ in partners.values():
+        late = late + jnp.where(early, 0, 1)
+
+        @pl.when(early)
+        def _(dev=dev):
+            pl.semaphore_signal(barrier, inc=1, device_id=dev, device_id_type=MESH)
 
     loads = [
         pltpu.make_async_copy(src, dst, local.at[i])
@@ -166,7 +191,17 @@
 
     started = []
 
-    def send(ref, dev, sems, i):
+    greeted = set()
+
+    def send(ref, name, sems, i):
+        dev, early, _ = partners[name]
+        if name not in greeted:
+            greeted.add(name)
+
+            @pl.when(early)
+            def _():
+                pl.semaphore_wait(ready.at[slots[name]], 1)
+
         copy = pltpu.make_async_remote_copy(
             src_ref=ref, dst_ref=ref, send_sem=sems[0].at[i], recv_sem=sems[1].at[i],
             device_id=dev, device_id_type=MESH,
@@ -183,22 +218,30 @@
     sx, sa, sb = (xs, xr), (as_, ar), (bs, br)
     lo, hi = pl.ds(0, 2), pl.ds(2, 2)
 
-    pl.semaphore_wait(barrier, len(peers))
-
-    send(bta.at[y, zl, xx], dev_zl, sa, 0)
-    send(btb.at[xx, zl, y], dev_zl, sb, 0)
-    send(xg.at[zh, core, lo], dev_zn, sx, 0)
-    send(xg.at[zh, core, hi], dev_zp, sx, 1)
-    send(xg.at[zh, core, hi], dev_zn, sx, 2)
-    send(xg.at[zh, core, lo], dev_zp, sx, 3)
-    send(xg.at[zh, core], dev_sib, sx, 4)
+    @pl.when(late > 0)
+    def _():
+        pl.semaphore_wait(barrier, late)
+
+    for dev, early, slot in partners.values():
+
+        @pl.when(jnp.logical_not(early))
+        def _(dev=dev, slot=slot):
+            pl.semaphore_signal(ready.at[slot], inc=1, device_id=dev, device_id_type=MESH)
+
+    send(bta.at[y, zl, xx], "zl", sa, 0)
+    send(btb.at[xx, zl, y], "zl", sb, 0)
+    send(xg.at[zh, core, lo], "zn", sx, 0)
+    send(xg.at[zh, core, hi], "zp", sx, 1)
+    send(xg.at[zh, core, hi], "zn", sx, 2)
+    send(xg.at[zh, core, lo], "zp", sx, 3)
+    send(xg.at[zh, core], "sib", sx, 4)
 
     arrive(bta.at[y, 1 - zl, xx], sa, 0)
-    send(bta.at[y, :, xx], dev_xn, sa, 1)
-    send(bta.at[y, :, xx], dev_xp, sa, 2)
+    send(bta.at[y, :, xx], "xn", sa, 1)
+    send(bta.at[y, :, xx], "xp", sa, 2)
     arrive(btb.at[xx, 1 - zl, y], sb, 0)
-    send(btb.at[xx, :, y], dev_yn, sb, 1)
-    send(btb.at[xx, :, y], dev_yp, sb, 2)
+    send(btb.at[xx, :, y], "yn", sb, 1)
+    send(btb.at[xx, :, y], "yp", sb, 2)
 
     loads[3].wait()
     loads[4].wait()
@@ -210,13 +253,13 @@
                 vt[slot, s, p, 2 * HEAD :] = ones
 
     arrive(bta.at[y, :, x_prev], sa, 1)
-    send(bta.at[y, 0, x_prev], dev_xn, sa, 3)
+    send(bta.at[y, 0, x_prev], "xn", sa, 3)
     arrive(bta.at[y, :, x_next], sa, 2)
-    send(bta.at[y, 1, x_next], dev_xp, sa, 4)
+    send(bta.at[y, 1, x_next], "xp", sa, 4)
     arrive(btb.at[xx, :, y_prev], sb, 1)
-    send(btb.at[xx, :, y_prev], dev_yn, sb, 3)
+    send(btb.at[xx, :, y_prev], "yn", sb, 3)
     arrive(btb.at[xx, :, y_next], sb, 2)
-    send(btb.at[xx, :, y_next], dev_yp, sb, 4)
+    send(btb.at[xx, :, y_next], "yp", sb, 4)
 
     loads[5].wait()
     loads[6].wait()
@@ -224,56 +267,56 @@
     x_opp = mod(xx + 2, NX)
     arrive(bta.at[y, 0, x_opp], sa, 3)
     arrive(bta.at[y, 1, x_opp], sa, 4)
-    send(bta.at[y], dev_yn, sa, 5)
-    send(bta.at[y], dev_yp, sa, 6)
+    send(bta.at[y], "yn", sa, 5)
+    send(bta.at[y], "yp", sa, 6)
     query_side(lambda s: xg[zh, core, s], wq, wg, qz, gt)
 
     y_prev2, y_next2 = mod(y - 2, NY), mod(y + 2, NY)
     y_prev3, y_next3 = mod(y - 3, NY), mod(y + 3, NY)
     y_opp = mod(y + 4, NY)
     arrive(btb.at[xx, :, y_prev2], sb, 3)
-    send(btb.at[xx, :, y_prev2], dev_yn, sb, 5)
+    send(btb.at[xx, :, y_prev2], "yn", sb, 5)
     arrive(btb.at[xx, :, y_next2], sb, 4)
-    send(btb.at[xx, :, y_next2], dev_yp, sb, 6)
+    send(btb.at[xx, :, y_next2], "yp", sb, 6)
     key_side(xg, zh, core, 0, 0, wk, wvt, kbuf, vt)
     arrive(btb.at[xx, :, y_prev3], sb, 5)
-    send(btb.at[xx, 0, y_prev3], dev_yn, sb, 7)
+    send(btb.at[xx, 0, y_prev3], "yn", sb, 7)
     arrive(btb.at[xx, :, y_next3], sb, 6)
-    send(btb.at[xx, 1, y_next3], dev_yp, sb, 8)
+    send(btb.at[xx, 1, y_next3], "yp", sb, 8)
     arrive(bta.at[y_prev], sa, 5)
-    send(bta.at[y_prev], dev_yn, sa, 7)
+    send(bta.at[y_prev], "yn", sa, 7)
     arrive(bta.at[y_next], sa, 6)
-    send(bta.at[y_next], dev_yp, sa, 8)
+    send(bta.at[y_next], "yp", sa, 8)
     arrive(btb.at[xx, 0, y_opp], sb, 7)
     arrive(btb.at[xx, 1, y_opp], sb, 8)
-    send(btb.at[xx], dev_xn, sb, 9)
-    send(btb.at[xx], dev_xp, sb, 10)
+    send(btb.at[xx], "xn", sb, 9)
+    send(btb.at[xx], "xp", sb, 10)
 
     arrive(xg.at[z_prev, core, lo], sx, 0)
-    send(xg.at[z_prev, core, lo], dev_zn, sx, 5)
-    send(xg.at[z_prev, core, lo], dev_sib, sx, 7)
+    send(xg.at[z_prev, core, lo], "zn", sx, 5)
+    send(xg.at[z_prev, core, lo], "sib", sx, 7)
     arrive(xg.at[z_next, core, hi], sx, 1)
-    send(xg.at[z_next, core, hi], dev_zp, sx, 6)
-    send(xg.at[z_next, core, hi], dev_sib, sx, 8)
+    send(xg.at[z_next, core, hi], "zp", sx, 6)
+    send(xg.at[z_next, core, hi], "sib", sx, 8)
     arrive(bta.at[y_prev2], sa, 7)
-    send(bta.at[y_prev2], dev_yn, sa, 9)
+    send(bta.at[y_prev2], "yn", sa, 9)
     arrive(bta.at[y_next2], sa, 8)
-    send(bta.at[y_next2], dev_yp, sa, 10)
+    send(bta.at[y_next2], "yp", sa, 10)
     arrive(xg.at[zh, 1 - core], sx, 4)
     key_side(xg, zh, 1 - core, 1, 0, wk, wvt, kbuf, vt)
     arrive(bta.at[y_prev3], sa, 9)
-    send(bta.at[y_prev3, 0], dev_yn, sa, 11)
+    send(bta.at[y_prev3, 0], "yn", sa, 11)
     arrive(bta.at[y_next3], sa, 10)
-    send(bta.at[y_next3, 1], dev_yp, sa, 12)
+    send(bta.at[y_next3, 1], "yp", sa, 12)
     arrive(btb.at[x_prev], sb, 9)
-    send(btb.at[x_prev, 0], dev_xn, sb, 11)
+    send(btb.at[x_prev, 0], "xn", sb, 11)
     arrive(btb.at[x_next], sb, 10)
-    send(btb.at[x_next, 1], dev_xp, sb, 12)
+    send(btb.at[x_next, 1], "xp", sb, 12)
 
     arrive(xg.at[z_prev, core, hi], sx, 2)
-    send(xg.at[z_prev, core, hi], dev_sib, sx, 9)
+    send(xg.at[z_prev, core, hi], "sib", sx, 9)
     arrive(xg.at[z_next, core, lo], sx, 3)
-    send(xg.at[z_next, core, lo], dev_sib, sx, 10)
+    send(xg.at[z_next, core, lo], "sib", sx, 10)
     key_side(xg, z_prev, core, 0, 1, wk, wvt, kbuf, vt)
     key_side(xg, z_next, core, 0, 2, wk, wvt, kbuf, vt)
     arrive(xg.at[z_prev, 1 - core, lo], sx, 7)
@@ -292,9 +335,9 @@
     attend(0, zh, core, True, pairs, *state)
     z_opp = mod(zh + 2, NZH)
     arrive(xg.at[z_opp, core, lo], sx, 5)
-    send(xg.at[z_opp, core, lo], dev_sib, sx, 11)
+    send(xg.at[z_opp, core, lo], "sib", sx, 11)
     arrive(xg.at[z_opp, core, hi], sx, 6)
-    send(xg.at[z_opp, core, hi], dev_sib, sx, 12)
+    send(xg.at[z_opp, core, hi], "sib", sx, 12)
     attend(1, z_prev, core, False, pairs, *state)
     attend(2, z_next, core, False, pairs, *state)
     key_side(xg, z_opp, core, 0, 3, wk, wvt, kbuf, vt)
@@ -328,7 +371,7 @@
         pltpu.VMEM((SEQS, PAIRS, 1, BLOCK), F32),
         pltpu.VMEM((SEQS, PAIRS, 1, BLOCK), F32),
         pltpu.VMEM((SEQS, PAIRS, 2, HEAD, ROWS), F32),
-        sem((8,)),
+        sem((8,)), pltpu.SemaphoreType.REGULAR((8,)),
         sem((13,)), sem((13,)), sem((13,)), sem((13,)), sem((13,)), sem((13,)),
     ]
 
@@ -342,7 +385,7 @@
         out_specs=pl.BlockSpec(memory_space=pltpu.VMEM),
         scratch_shapes=scratch(),
         compiler_params=pltpu.CompilerParams(
-            collective_id=0, has_side_effects=True, vmem_limit_bytes=48 * 1024 * 1024
+            collective_id=0, has_side_effects=True, vmem_limit_bytes=63 * 1024 * 1024
         ),
         cost_estimate=pl.CostEstimate(flops=6 * 10**9, bytes_accessed=2 * 10**6, transcendentals=5 * 10**6),
     )(x, gain.reshape(1, -1), wq, wk, wv, wg, wo, jnp.swapaxes(b, 1, 2))

time: 75.6 us -> 52.7 us (0.70)
  the two profiles are of different devices: /device:TPU:16 before, /device:TPU:8 now
where the time goes in v2:
time: 52.7 us; the launch traced here: 52.6 us
  Pallas kernels  50.9 us (97%)
  local copies, waits for them, and re-layouts  1.67 us (3%)
    pallas_call x1, Pallas kernels, on_device(): pl.pallas_call(kernel, out_shape=jax.ShapeDtypeStruct(x.shape, x.dtype),...  50.9 us
    unnamed x1, local copies, waits for them, and re-layouts  1.67 us

profile of v2, /device:TPU:8, one launch (start us, length us, event | category | flops | bytes accessed | tf_op | source)
XLA Modules:
  0.0 52.6 jit_solution(18010372831238072012)
XLA Ops:
  0.0 50.9 %shard_map.82 = bf16[4,128,256]{2,1,0:T(8,128)(2,1)} custom-call(bf16[4,128,256]{2,1,0:T(8,128)(2,1)} %x_hbm.1, f32[1,256]{1,0:T(1,128)} %bitcast.3, bf16[256,256]{1,0:T(8,128)(2,1)} %wq_hbm.1, bf16[256,256]{1,0:T(8,128)(2,1)} %wk_hbm.1, bf16[256,256]{1,0:T(8,128)(2,1)} %wv_hbm.1, bf16[256,256]{1,0:T(8,128)(2,1)} %wg_hbm.1, bf16[256,256]{1,0:T(8,128)(2,1)} %wo_hbm.1, ...), custom_call_target="tpu_custom_call" | custom-call | flops 6000000000 | bytes 2000000 | tf_op jit(solution)/shard_map/pallas_call | solution.py:381
  50.9 1.7 %copy.10 = bf16[4,128,256]{2,1,0:T(8,128)(2,1)} copy(bf16[4,128,256]{2,1,0:T(8,128)(2,1)} %shard_map.82) | data formatting | bytes 524288

commit v3 on v2

v3 whole, which is shorter than its diff:
```python
import functools

import jax
import jax.numpy as jnp
from jax import lax
from jax.experimental import pallas as pl
from jax.experimental.pallas import tpu as pltpu
from jax.sharding import PartitionSpec as P

MESH = pl.DeviceIdType.MESH
BF16, F32 = jnp.bfloat16, jnp.float32
SEQS, ROWS, WIDTH, HEADS, HEAD = 4, 128, 256, 8, 32
PAIRS, BLOCK = HEADS // 2, 2 * ROWS
NX, NY, NZL, NZH = 4, 8, 2, 4
AUG = 80
FIRST = 3
COPIES = 80
TA, TB, TX, EN, EP = 4.0, 1.5, (7.5, 10.0), 2.2, 5.0
TL = {"zn": (7.5, 10.0), "zp": (7.5, 10.0)}


def dot(a, b):
    return jnp.dot(a, b, preferred_element_type=F32)


def dot_nt(a, b):
    return lax.dot_general(a, b, (((1,), (1,)), ((), ())), preferred_element_type=F32)


def normalise(rows, gain):
    wide = rows.astype(F32)
    center = jnp.mean(wide, axis=-1, keepdims=True)
    moved = wide - center
    variance = jnp.mean(moved * moved, axis=-1, keepdims=True)
    return (moved * lax.rsqrt(variance + 1e-05) * gain).astype(BF16)


def query_side(xn, wq, wg, qz, gt):
    wqt, wgt = wq[...].T, wg[...].T
    qz[...] = jnp.zeros_like(qz)
    for s in range(SEQS):
        rows = xn(s)
        qt = (dot_nt(wqt, rows) * HEAD**-0.5).astype(BF16)
        for h in range(HEADS):
            p, half = h // 2, h % 2
            qz[s, p, h * HEAD : (h + 1) * HEAD, half * ROWS : (half + 1) * ROWS] = qt[
                h * HEAD : (h + 1) * HEAD
            ]
        gt[s] = jax.nn.sigmoid(dot_nt(wgt, rows))


def key_side(xg, zh, core, c, slot, wk, wvt, kbuf, vt):
    wvt_all = wvt[...]
    for s in range(SEQS):
        rows = xg[zh, core, s]
        kbuf[slot, s, c * ROWS : (c + 1) * ROWS, :] = dot(rows, wk[...]).astype(BF16)
        values = dot_nt(wvt_all, rows).astype(BF16)
        for p in range(PAIRS):
            vt[slot, s, p, : 2 * HEAD, c * ROWS : (c + 1) * ROWS] = values[
                2 * HEAD * p : 2 * HEAD * (p + 1)
            ]


def bias_block(bta, btb, h, zl, ys):
    pieces = []
    for y in ys:
        for x in range(NX):
            if h < FIRST:
                pieces.append(bta[y, zl, x, h])
            else:
                pieces.append(btb[x, zl, y, h - FIRST])
    return jnp.concatenate(pieces, axis=0).astype(F32)


def attend(slot, zh, core, first, pairs, kbuf, vt, qz, bta, btb, m_ref, l_ref, acc):
    zl = zh // (NZH // NZL)
    y0 = lax.rem(zh, NZH // NZL) * (NY // 2)
    ys = [y0 + 2 * core, y0 + 2 * core + 1, y0 + 2 * (1 - core), y0 + 2 * (1 - core) + 1]

    def bias(p):
        return jnp.concatenate([bias_block(bta, btb, 2 * p + i, zl, ys) for i in range(2)], axis=1)

    def run(items):
        n = len(items)
        old, sc, w = [None] * n, [None] * n, [None] * n

        def one(i):
            s, p = items[i]
            old[i] = None if first else (m_ref[s, p], l_ref[s, p], acc[s, p, 0], acc[s, p, 1])
            sc[i] = dot(kbuf[slot, s], qz[s, p])

        def two(i):
            s, p = items[i]
            scores = sc[i] + bias(p)
            top = jnp.max(scores, axis=0, keepdims=True)
            if not first:
                top = jnp.maximum(old[i][0], top)
            w[i] = (top, jnp.exp(scores - top).astype(BF16))

        def three(i):
            s, p = items[i]
            top, weights = w[i]
            mixed = dot(vt[slot, s, p], weights)
            total = mixed[2 * HEAD : 2 * HEAD + 1]
            left, right = mixed[:HEAD, :ROWS], mixed[HEAD : 2 * HEAD, ROWS:]
            if not first:
                scale = jnp.exp(old[i][0] - top)
                total = old[i][1] * scale + total
                left = old[i][2] * scale[:, :ROWS] + left
                right = old[i][3] * scale[:, ROWS:] + right
            m_ref[s, p], l_ref[s, p], acc[s, p, 0], acc[s, p, 1] = top, total, left, right

        for t in range(n + 4):
            if t < n:
                one(t)
            if 0 <= t - 2 < n:
                two(t - 2)
            if 0 <= t - 4 < n:
                three(t - 4)

    run([(s, p) for s in range(SEQS) for p in pairs])


def finish(wo, gt, l_ref, acc, held, out, sems):
    copies = []
    for s in range(SEQS):
        parts = []
        for p in range(PAIRS):
            for half in range(2):
                h = 2 * p + half
                total = l_ref[s, p, :, half * ROWS : (half + 1) * ROWS]
                parts.append(acc[s, p, half] / total * gt[s, h * HEAD : (h + 1) * HEAD])
        gated = jnp.concatenate(parts, axis=0).astype(BF16)
        held[s] = dot(gated.T, wo[...]).astype(BF16)
        copies.append(pltpu.make_async_copy(held.at[s], out.at[s], sems.at[s]))
        copies[-1].start()
    for copy in copies:
        copy.wait()


def kernel(
    x_hbm, gain_hbm, wq_hbm, wk_hbm, wv_hbm, wg_hbm, wo_hbm, b_hbm, out,
    x, gain, wq, wk, wv, wg, wo, b,
    xg, bta, btb, wvt, kbuf, vt, qz, gt, m_ref, l_ref, acc,
    local, ready, sent, received,
):
    seq, res = lax.axis_index("seq"), lax.axis_index("res")
    zl, y, xx = seq // (NY * NX), lax.rem(seq // NX, NY), lax.rem(seq, NX)
    zh, core = res // 2, lax.rem(res, 2)

    def at_seq(zl_, y_, x_):
        return (zl_ * (NY * NX) + y_ * NX + x_, res)

    def at_res(zh_, core_):
        return (seq, zh_ * 2 + core_)

    def mod(v, n):
        return lax.rem(v + n, n)

    def y_at(k):
        return mod(y + k, NY)

    z_next, z_prev, z_opp = mod(zh + 1, NZH), mod(zh - 1, NZH), mod(zh + 2, NZH)
    y_next, y_prev = y_at(1), y_at(-1)
    x_next, x_prev, x_opp = mod(xx + 1, NX), mod(xx - 1, NX), mod(xx + 2, NX)
    z_side = (zl, 1 - zl)

    barrier = pltpu.get_barrier_semaphore()
    partners = {
        "zn": (at_res(z_next, core), zh < z_next, 1),
        "zp": (at_res(z_prev, core), zh < z_prev, 0),
        "sib": (at_res(zh, 1 - core), core < 1, 2),
        "yn": (at_seq(zl, y_next, xx), y < y_next, 4),
        "yp": (at_seq(zl, y_prev, xx), y < y_prev, 3),
        "xn": (at_seq(zl, y, x_next), xx < x_next, 6),
        "xp": (at_seq(zl, y, x_prev), xx < x_prev, 5),
        "xo": (at_seq(zl, y, x_opp), xx < x_opp, 7),
        "zl": (at_seq(1 - zl, y, xx), zl < 1, 8),
    }
    slots = {name: i for i, name in enumerate(partners)}
    late = 0
    for dev, early, _ in partners.values():
        late = late + jnp.where(early, 0, 1)

        @pl.when(early)
        def _(dev=dev):
            pl.semaphore_signal(barrier, inc=1, device_id=dev, device_id_type=MESH)

    loads = [
        pltpu.make_async_copy(src, dst, local.at[i])
        for i, (src, dst) in enumerate(
            [(x_hbm, x), (gain_hbm, gain), (b_hbm, b), (wk_hbm, wk), (wv_hbm, wv), (wq_hbm, wq), (wg_hbm, wg), (wo_hbm, wo)]
        )
    ]
    for load in loads:
        load.start()
    @pl.when(late > 0)
    def _():
        pl.semaphore_wait(barrier, late)

    for dev, early, slot in partners.values():

        @pl.when(jnp.logical_not(early))
        def _(dev=dev, slot=slot):
            pl.semaphore_signal(ready.at[slot], inc=1, device_id=dev, device_id_type=MESH)

    loads[0].wait()
    loads[1].wait()
    for s in range(SEQS):
        xg[zh, core, s] = normalise(x[s], gain[...])
    loads[2].wait()
    bta[y, zl, xx] = b[:FIRST]
    btb[xx, zl, y] = b[FIRST:]

    started, greeted, numbers = [], set(), {}

    def copy_of(key, ref, name):
        i = numbers.setdefault(key, len(numbers))
        return pltpu.make_async_remote_copy(
            src_ref=ref, dst_ref=ref, send_sem=sent.at[i], recv_sem=received.at[i],
            device_id=partners[name][0], device_id_type=MESH,
        )

    def greet(name):
        if name not in greeted:
            greeted.add(name)

            @pl.when(partners[name][1])
            def _():
                pl.semaphore_wait(ready.at[slots[name]], 1)

    def send(key, ref, name):
        greet(name)
        copy = copy_of(key, ref, name)
        copy.start()
        started.append(copy)

    def arrive(key, ref):
        copy_of(key, ref, "sib").wait_recv()

    plan = []

    def at(time):
        def add(step):
            plan.append((time, len(plan), step))
            return step

        return add

    across = (("xn", x_prev), ("xp", x_next), ("xo", x_opp))

    @at(0)
    def _():
        send(("bz",), btb.at[xx, zl, y], "zl")
        send(("az",), bta.at[y, zl, xx], "zl")
        for name, _ in across:
            send(("ax", 0, name), bta.at[y, zl, xx], name)

    @at(1.31)
    def _():
        arrive(("az",), bta.at[y, 1 - zl, xx])
        for name, _ in across:
            send(("ax", 1, name), bta.at[y, 1 - zl, xx], name)

    for half in range(2):

        @at(1.5 + 1.3 * half)
        def _(half=half):
            for name, origin in across:
                arrive(("ax", half, name), bta.at[y, z_side[half], origin])
            for name in ("yn", "yp"):
                send(("ay", 0, half, name), bta.at[y, z_side[half]], name)

        for k in range(1, 4):

            @at(TA + 2.2 * (k - 1) + 1.1 * half)
            def _(k=k, half=half):
                for name, step, far in (("yn", -k, 0), ("yp", k, 1)):
                    slab = bta.at[y_at(step), z_side[half]]
                    arrive(("ay", k - 1, half, name), slab)
                    if k < 3 or half == far:
                        send(("ay", k, half, name), slab, name)

    @at(TA + 7.4)
    def _():
        arrive(("ay", 3, 0, "yn"), bta.at[y_at(4), z_side[0]])
        arrive(("ay", 3, 1, "yp"), bta.at[y_at(4), z_side[1]])

    def spread(k):
        for name in ("xn", "xp"):
            send(("bx", k, name), btb.at[xx, :, y_at(k)], name)

    @at(1.3)
    def _():
        arrive(("bz",), btb.at[xx, 1 - zl, y])
        for name in ("yn", "yp"):
            send(("by", 0, name), btb.at[xx, :, y], name)
        spread(0)

    for k in range(1, 4):

        @at(1.3 + TB * k)
        def _(k=k):
            for name, step, far in (("yn", -k, 0), ("yp", k, 1)):
                slab = btb.at[xx, :, y_at(step)]
                arrive(("by", k - 1, name), slab)
                send(("by", k, name), slab if k < 3 else btb.at[xx, z_side[far], y_at(step)], name)
            spread(-k)
            spread(k)

    @at(1.3 + TB * 4)
    def _():
        arrive(("by", 3, "yn"), btb.at[xx, z_side[0], y_at(4)])
        arrive(("by", 3, "yp"), btb.at[xx, z_side[1], y_at(4)])
        spread(4)

    order = (0, -1, 1, -2, 2, -3, 3, 4)
    for i, k in enumerate(order):

        @at(max(2.9 + 0.85 * i, 1.4 + TB * abs(k) + 1.4))
        def _(i=i, k=k):
            arrive(("bx", k, "xn"), btb.at[x_prev, :, y_at(k)])
            arrive(("bx", k, "xp"), btb.at[x_next, :, y_at(k)])
            if i in (0, 1, 4, 5):
                send(("bo", k), btb.at[x_prev, :, y_at(k)], "xn")
            else:
                send(("bo", k), btb.at[x_next, :, y_at(k)], "xp")

    @at(11.9)
    def _():
        for k in order:
            arrive(("bo", k), btb.at[x_opp, :, y_at(k)])

    halves = (slice(0, SEQS // 2), slice(SEQS // 2, SEQS))
    first_half = {"zn": 0, "zp": 1}

    def rows_to(name, when_early):
        early = partners[name][1]
        greeted.add(name)
        copies = [
            copy_of(("xo", name, i), xg.at[zh, core, halves[first_half[name] ^ i]], name) for i in range(2)
        ]

        @pl.when(early if when_early else jnp.logical_not(early))
        def _():
            if when_early:
                pl.semaphore_wait(ready.at[slots[name]], 1)
            for copy in copies:
                copy.start()

        if when_early:
            started.extend(copies)

    at(0.01)(lambda: rows_to("zp", False))
    at(0.02)(lambda: rows_to("zn", False))
    at(0.03)(lambda: send(("xs",), xg.at[zh, core], "sib"))
    at(EN)(lambda: rows_to("zn", True))
    at(EP)(lambda: rows_to("zp", True))

    def rows_from(name, origin, i):
        part = xg.at[origin, core, halves[first_half[name] ^ i]]
        onward = [copy_of(("xt", name, i), part, "sib")]
        if i == 0:
            onward.append(copy_of(("xf", name), part, name))
        started.extend(onward)
        come = copy_of(("xo", name, i), part, "sib")

        def step():
            come.wait_recv()
            for copy in onward:
                copy.start()

        at(TX[i])(lambda: pl.when(zh >= 2)(step))
        at(TL[name][i])(lambda: pl.when(zh < 2)(step))

    for name, origin in (("zn", z_prev), ("zp", z_next)):
        for i in range(2):
            rows_from(name, origin, i)

    def rows_told(name, origin, i):
        arrive(("xt", name, i), xg.at[origin, 1 - core, halves[first_half[name] ^ i]])

    state = (kbuf, vt, qz, bta, btb, m_ref, l_ref, acc)
    pairs = range(PAIRS)

    @at(0.04)
    def _():
        loads[3].wait()
        loads[4].wait()
        wvt[...] = wv[...].T
        ones = jnp.ones((AUG - 2 * HEAD, BLOCK), BF16)
        for slot in range(NZH):
            for s in range(SEQS):
                for p in range(PAIRS):
                    vt[slot, s, p, 2 * HEAD :] = ones

    @at(1.7)
    def _():
        loads[5].wait()
        loads[6].wait()
        query_side(lambda s: xg[zh, core, s], wq, wg, qz, gt)

    at(3.1)(lambda: key_side(xg, zh, core, 0, 0, wk, wvt, kbuf, vt))

    @at(6.1)
    def _():
        arrive(("xs",), xg.at[zh, 1 - core])
        key_side(xg, zh, 1 - core, 1, 0, wk, wvt, kbuf, vt)

    for slot, (name, origin) in enumerate((("zn", z_prev), ("zp", z_next)), start=1):

        @at(14.1)
        def _(slot=slot, origin=origin):
            key_side(xg, origin, core, 0, slot, wk, wvt, kbuf, vt)

        @at(14.2)
        def _(slot=slot, name=name, origin=origin):
            rows_told(name, origin, 0)
            rows_told(name, origin, 1)
            key_side(xg, origin, 1 - core, 1, slot, wk, wvt, kbuf, vt)

    at(15.0)(lambda: attend(0, zh, core, True, pairs, *state))
    at(15.2)(lambda: attend(1, z_prev, core, False, pairs, *state))

    @at(15.3)
    def _():
        for name in ("zn", "zp"):
            part = xg.at[z_opp, core, halves[first_half[name]]]
            arrive(("xf", name), part)
            send(("xu", name), part, "sib")

    at(15.4)(lambda: attend(2, z_next, core, False, pairs, *state))

    @at(15.5)
    def _():
        key_side(xg, z_opp, core, 0, 3, wk, wvt, kbuf, vt)
        for name in ("zn", "zp"):
            arrive(("xu", name), xg.at[z_opp, 1 - core, halves[first_half[name]]])
        key_side(xg, z_opp, 1 - core, 1, 3, wk, wvt, kbuf, vt)

    at(15.6)(lambda: attend(3, z_opp, core, False, pairs, *state))
    loads_left = loads[7]

    for _, _, step in sorted(plan, key=lambda entry: entry[:2]):
        step()
    loads_left.wait()
    finish(wo, gt, l_ref, acc, x, out, local)
    for copy in started:
        copy.wait_send()


def scratch():
    sem = pltpu.SemaphoreType.DMA
    mat = pltpu.VMEM((WIDTH, WIDTH), BF16)
    return [
        pltpu.VMEM((SEQS, ROWS, WIDTH), BF16),
        pltpu.VMEM((1, WIDTH), F32),
        mat, mat, mat, mat, mat,
        pltpu.VMEM((HEADS, 16, ROWS), BF16),
        pltpu.VMEM((NZH, 2, SEQS, ROWS, WIDTH), BF16),
        pltpu.VMEM((NY, NZL, NX, FIRST, 16, ROWS), BF16),
        pltpu.VMEM((NX, NZL, NY, HEADS - FIRST, 16, ROWS), BF16),
        mat,
        pltpu.VMEM((NZH, SEQS, BLOCK, WIDTH), BF16),
        pltpu.VMEM((NZH, SEQS, PAIRS, AUG, BLOCK), BF16),
        pltpu.VMEM((SEQS, PAIRS, WIDTH, BLOCK), BF16),
        pltpu.VMEM((SEQS, WIDTH, ROWS), F32),
        pltpu.VMEM((SEQS, PAIRS, 1, BLOCK), F32),
        pltpu.VMEM((SEQS, PAIRS, 1, BLOCK), F32),
        pltpu.VMEM((SEQS, PAIRS, 2, HEAD, ROWS), F32),
        sem((8,)), pltpu.SemaphoreType.REGULAR((9,)),
        sem((COPIES,)), sem((COPIES,)),
    ]


def on_device(x, gain, wq, wk, wv, wg, wo, b):
    any_space = pl.BlockSpec(memory_space=pltpu.HBM)
    return pl.pallas_call(
        kernel,
        out_shape=jax.ShapeDtypeStruct(x.shape, x.dtype),
        in_specs=[any_space] * 8,
        out_specs=any_space,
        scratch_shapes=scratch(),
        compiler_params=pltpu.CompilerParams(
            collective_id=0, has_side_effects=True, vmem_limit_bytes=63 * 1024 * 1024
        ),
        cost_estimate=pl.CostEstimate(flops=6 * 10**9, bytes_accessed=2 * 10**6, transcendentals=5 * 10**6),
    )(x, gain.reshape(1, -1), wq, wk, wv, wg, wo, jnp.swapaxes(b, 1, 2))


def solution(mesh):
    return jax.shard_map(
        on_device,
        mesh=mesh,
        in_specs=(P("seq", "res", None), P(), P(), P(), P(), P(), P(), P(None, "res", "seq")),
        out_specs=P("seq", "res", None),
        check_vma=False,
    )
```

time: 52.7 us -> 46.4 us (0.88)
  Pallas kernels: 50.9 us -> 44.6 us
    pallas_call x1, Pallas kernels: 50.9 us -> 44.6 us  [on_device(): pl.pallas_call(kernel, out_shape=jax.ShapeDtypeStruct(x.shape, x.dtype),...]
where the time goes in v3:
time: 46.4 us; the launch traced here: 46.3 us
  Pallas kernels  44.6 us (96%)
  local copies, waits for them, and re-layouts  1.67 us (4%)
    pallas_call x1, Pallas kernels, on_device(): pl.pallas_call(kernel, out_shape=jax.ShapeDtypeStruct(x.shape, x.dtype),...  44.6 us
    unnamed x1, local copies, waits for them, and re-layouts  1.67 us

profile of v3, /device:TPU:8, one launch (start us, length us, event | category | flops | bytes accessed | tf_op | source)
XLA Modules:
  0.0 46.3 jit_solution(16655351587826743870)
XLA Ops:
  0.0 44.6 %shard_map.82 = bf16[4,128,256]{2,1,0:T(8,128)(2,1)} custom-call(bf16[4,128,256]{2,1,0:T(8,128)(2,1)} %x_hbm.1, f32[1,256]{1,0:T(1,128)} %bitcast.3, bf16[256,256]{1,0:T(8,128)(2,1)} %wq_hbm.1, bf16[256,256]{1,0:T(8,128)(2,1)} %wk_hbm.1, bf16[256,256]{1,0:T(8,128)(2,1)} %wv_hbm.1, bf16[256,256]{1,0:T(8,128)(2,1)} %wg_hbm.1, bf16[256,256]{1,0:T(8,128)(2,1)} %wo_hbm.1, ...), custom_call_target="tpu_custom_call" | custom-call | flops 6000000000 | bytes 2000000 | tf_op jit(solution)/shard_map/pallas_call | solution.py:478
  44.6 1.7 %copy.10 = bf16[4,128,256]{2,1,0:T(8,128)(2,1)} copy(bf16[4,128,256]{2,1,0:T(8,128)(2,1)} %shard_map.82) | data formatting | bytes 524288

commit v4 on v3

--- a/solution.py
+++ b/solution.py
@@ -351,8 +351,8 @@
         if when_early:
             started.extend(copies)
 
-    at(0.01)(lambda: rows_to("zp", False))
-    at(0.02)(lambda: rows_to("zn", False))
+    at(1.32)(lambda: rows_to("zp", False))
+    at(1.33)(lambda: rows_to("zn", False))
     at(0.03)(lambda: send(("xs",), xg.at[zh, core], "sib"))
     at(EN)(lambda: rows_to("zn", True))
     at(EP)(lambda: rows_to("zp", True))

time: 46.4 us -> 45.3 us (0.976)
  the two profiles are of different devices: /device:TPU:8 before, /device:TPU:1 now
where the time goes in v4:
time: 45.3 us; the launch traced here: 45.1 us
  Pallas kernels  43.4 us (96%)
  local copies, waits for them, and re-layouts  1.67 us (4%)
    pallas_call x1, Pallas kernels, on_device(): pl.pallas_call(kernel, out_shape=jax.ShapeDtypeStruct(x.shape, x.dtype),...  43.4 us
    unnamed x1, local copies, waits for them, and re-layouts  1.67 us

profile of v4, /device:TPU:1, one launch (start us, length us, event | category | flops | bytes accessed | tf_op | source)
XLA Modules:
  0.0 45.1 jit_solution(12003661535763249936)
XLA Ops:
  0.0 43.4 %shard_map.82 = bf16[4,128,256]{2,1,0:T(8,128)(2,1)} custom-call(bf16[4,128,256]{2,1,0:T(8,128)(2,1)} %x_hbm.1, f32[1,256]{1,0:T(1,128)} %bitcast.3, bf16[256,256]{1,0:T(8,128)(2,1)} %wq_hbm.1, bf16[256,256]{1,0:T(8,128)(2,1)} %wk_hbm.1, bf16[256,256]{1,0:T(8,128)(2,1)} %wv_hbm.1, bf16[256,256]{1,0:T(8,128)(2,1)} %wg_hbm.1, bf16[256,256]{1,0:T(8,128)(2,1)} %wo_hbm.1, ...), custom_call_target="tpu_custom_call" | custom-call | flops 6000000000 | bytes 2000000 | tf_op jit(solution)/shard_map/pallas_call | solution.py:478
  43.4 1.7 %copy.10 = bf16[4,128,256]{2,1,0:T(8,128)(2,1)} copy(bf16[4,128,256]{2,1,0:T(8,128)(2,1)} %shard_map.82) | data formatting | bytes 524288
